TPU v7x, 1024 devices: a whole 8x8x8 slice. The times are simulated.
1024 devices in a mesh: rep: 16 (over x, y_hi), fsdp: 64 (over y_lo, z, core).
Axes of the slice: x: 8, y: 8 (y_hi: 2, y_lo: 4; y = y_hi * 4 + y_lo), z: 8, core: 2. Of those that a mesh axis runs over, the one named last changes fastest.
Arguments:
- tokens: bfloat16 [196608, 4096], P(('rep', 'fsdp')), may hold values from -24 to 24
- cotangent: bfloat16 [196608, 256], P(('rep', 'fsdp')), may hold values from -6 to 6
- weight: float32 [4096, 256], P('fsdp'), may hold values from -0.09375 to 0.09375
- momentum: float32 [16, 4096, 256], P('rep', 'fsdp'), may hold values from -6 to 6
- column_order: int32 [64], replicated, may hold values from 0 to 63, each once
Outputs:
- input_grad: bfloat16 [196608, 4096], P(('rep', 'fsdp'))
- new_momentum: float32 [16, 4096, 256], P('rep', 'fsdp')
- update: float32 [4096, 256], P('fsdp')
- new_weight: float32 [4096, 256], P('fsdp')
Inputs may be any that keep to these rules, and one draw needn't show every extreme that they name: `column_order`: each of the 64 frequency indices appears exactly once.
All inputs are finite; a program needn't handle non-finite values.
Results may differ from a plain program's by a relative error of at most 0.0049.
Values may be sent and summed in bfloat16 or wider, within the bound.
A program may use at most 32 MiB of HBM per device.

v0:
```python
import math

import jax
import jax.numpy as jnp
from jax import lax
from jax.sharding import PartitionSpec as P

KW = 256
BLOCK = 64
SEL = 16


MOMENTUM_DECAY = 0.9
LEARN_RATE = 0.05


def dct_table():
    index = jnp.arange(BLOCK).astype(jnp.float32)
    table = jnp.cos(
        math.pi * (2.0 * index[None, :] + 1.0) * index[:, None] / (2.0 * BLOCK)
    ) * math.sqrt(2.0 / BLOCK)
    return jnp.where(index[:, None] == 0.0, table * math.sqrt(0.5), table)


def on_device(tokens, cotangent, weight, momentum, column_order):
    members = lax.axis_size("fsdp")
    replicas = lax.axis_size("rep")
    rows_own = weight.shape[0]
    table = dct_table()
    weight_half = weight.astype(jnp.bfloat16)
    input_grad = lax.dot_general(
        cotangent,
        lax.all_gather(weight_half, "fsdp", axis=0, tiled=True),
        (((1,), (1,)), ((), ())),
        preferred_element_type=jnp.float32,
    ).astype(jnp.bfloat16)
    scale = float(tokens.shape[0] * members) ** (-0.5)
    weight_grad = (
        lax.psum_scatter(
            lax.dot_general(
                tokens, cotangent, (((0,), (0,)), ((), ())), preferred_element_type=jnp.float32
            ),
            "fsdp",
            scatter_dimension=0,
            tiled=True,
        )
        * scale
    )
    moment = MOMENTUM_DECAY * momentum[0] + weight_grad
    blocks = moment.reshape(rows_own // BLOCK, BLOCK, KW // BLOCK, BLOCK)
    coeffs = jnp.einsum("kn,anbm,lm->akbl", table, blocks, table, precision=lax.Precision.HIGHEST)
    picker = (jnp.arange(BLOCK)[:, None] == column_order[None, :SEL]).astype(jnp.float32)
    compact = jnp.einsum("akbl,ls->akbs", coeffs, picker, precision=lax.Precision.HIGHEST)
    sent = jnp.einsum("akbs,ls->akbl", compact, picker, precision=lax.Precision.HIGHEST)
    own_back = jnp.einsum("kn,akbl,lm->anbm", table, sent, table, precision=lax.Precision.HIGHEST)
    new_momentum = (moment - own_back.reshape(rows_own, KW))[None]
    flat_sent = compact.reshape(-1)
    gathered = lax.all_gather(flat_sent, "rep", axis=0, tiled=True)
    summed = jnp.sum(gathered.reshape(replicas, -1), axis=0)
    summed_full = jnp.einsum(
        "akbs,ls->akbl", summed.reshape(compact.shape), picker, precision=lax.Precision.HIGHEST
    )
    decoded = jnp.einsum(
        "kn,akbl,lm->anbm", table, summed_full, table, precision=lax.Precision.HIGHEST
    )
    update = decoded.reshape(rows_own, KW) / replicas
    new_weight = weight - LEARN_RATE * update
    return (input_grad, new_momentum, update, new_weight)


def solution(mesh):
    in_specs = (
        P(("rep", "fsdp"), None),
        P(("rep", "fsdp"), None),
        P("fsdp", None),
        P("rep", "fsdp", None),
        P(),
    )
    out_specs = (P(("rep", "fsdp"), None), P("rep", "fsdp", None), P("fsdp", None), P("fsdp", None))
    return jax.shard_map(
        on_device, mesh=mesh, in_specs=in_specs, out_specs=out_specs, check_vma=False
    )
```

profile of v0, /device:TPU:1, one launch (start us, length us, event | category | flops | bytes accessed | tf_op | source)
XLA Modules:
  0.0 495.6 jit_solution(15227841578337704923)
XLA Ops:
  7.2 0.0 copy-start
  7.2 0.0 reduce-scatter.2.cloned.1.call-start
  7.2 1.4 copy-done
  8.6 3.6 fusion.78
  12.2 0.0 copy-start.2
  12.2 0.0 copy-start.4
  12.2 0.0 reduce-scatter.2.cloned.1.call-update
  12.2 0.0 copy-start.3
  12.2 0.0 all-gather.2.cloned.1.call-start
  12.3 298.3 %reduce-scatter.2.cloned.1.call-done = f32[64,256]{1,0:T(8,128)} async-done(((f32[4096,256]{1,0:T(8,128)}), f32[64,256]{1,0:T(8,128)}) %reduce-scatter.2.cloned.1.call-update) | async-done | bytes 65552 | tf_op jit(solution)/shard_map/reduce_scatter | solution.py:39
  310.6 0.0 copy-done.2
  310.6 0.9 bitcast_add_fusion
  311.5 0.1 copy.41
  311.6 0.7 fusion.10
  312.2 0.4 convolution_bitcast_fusion.1
  312.7 0.0 copy-done.4
  312.7 0.3 fusion.52
  312.9 0.1 copy.30
  313.1 0.1 reshape.85
  313.2 44.2 %all_gather.7 = f32[65536]{0:T(1024)S(1)} all-gather(f32[4096]{0:T(1024)S(1)} %reshape.85), channel_id=1, replica_groups=mesh['rep'=16,'fsdp'=64] {'rep'}, dimensions={0}, use_global_device_ids=true | all-gather | bytes 278528 | tf_op jit(solution)/shard_map/all_gather | solution.py:58
  357.4 0.0 copy-start.1
  357.4 0.1 reshape.86
  357.5 0.1 reshape.87
  357.7 0.4 fusion
  358.1 0.7 fusion.4
  358.8 0.4 multiply_bitcast_fusion
  359.2 0.1 copy.35
  359.3 0.1 mul.167
  359.5 0.0 copy-done.3
  359.5 0.6 fusion.75
  360.1 0.0 all-gather.2.cloned.1.call-update
  360.1 0.3 fusion.50
  360.5 0.7 fusion.7
  361.1 0.4 convolution_bitcast_fusion
  361.6 0.1 copy.29
  361.7 0.1 reshape.84
  361.8 0.1 copy.34
  361.9 0.8 div.34
  362.7 0.6 subtract_bitcast_fusion
  363.3 121.9 %all-gather.2.cloned.1.call-done = bf16[4096,256]{1,0:T(8,128)(2,1)} async-done(((bf16[64,256]{1,0:T(8,128)(2,1)}), bf16[4096,256]{1,0:T(8,128)(2,1)}) %all-gather.2.cloned.1.call-update) | async-done | bytes 2097168 | tf_op jit(solution)/shard_map/all_gather | solution.py:33
  485.2 0.0 copy-done.1
  485.2 3.6 convolution_convert_fusion
  (4 shorter events, 0.1 us)
Async XLA Ops:
  7.2 1.4 copy-start
  7.2 303.4 %reduce-scatter.2.cloned.1.call-start = ((), (), s32[]{:S(2)}) async-start(), calls=%async_computation.2 | async-start | bytes 4259840 | tf_op jit(solution)/shard_map/reduce_scatter | solution.py:39
  12.2 298.4 %copy-start.2 = (f32[1,64,256]{2,1,0:T(8,128)S(1)}, f32[1,64,256]{2,1,0:T(8,128)}, u32[]{:S(2)}) copy-start(f32[1,64,256]{2,1,0:T(8,128)} %param.8) | copy-start | bytes 196612
  12.2 300.5 %copy-start.4 = (s32[64]{0:T(128)S(1)}, s32[64]{0:T(128)}, u32[]{:S(2)}) copy-start(s32[64]{0:T(128)} %param.9) | copy-start | bytes 772
  12.2 347.2 %copy-start.3 = (f32[64,256]{1,0:T(8,128)S(1)}, f32[64,256]{1,0:T(8,128)}, u32[]{:S(2)}) copy-start(f32[64,256]{1,0:T(8,128)} %param.7) | copy-start | bytes 196612
  12.2 473.0 %all-gather.2.cloned.1.call-start = ((), (), s32[]{:S(2)}) async-start(), calls=%async_computation.1 | async-start | bytes 2129920 | tf_op jit(solution)/shard_map/all_gather | solution.py:33
  357.4 127.8 %copy-start.1 = (bf16[192,256]{1,0:T(8,128)(2,1)S(1)}, bf16[192,256]{1,0:T(8,128)(2,1)}, u32[]{:S(2)}) copy-start(bf16[192,256]{1,0:T(8,128)(2,1)} %param.6) | copy-start | bytes 294916
Sparse Core Ops, SparseCore 0:
  12.3 298.2 reduce-scatter.1
  360.2 124.9 all-gather.1
where the time goes:
time: 496 us
  waiting for transfers between devices  420 us (85%)
  blocking collectives  44.2 us (9%)
  between operations  14.2 us (3%)
  matrix products  11.5 us (2%)
    reduce_scatter x1, waiting for transfers between devices, on_device(): lax.psum_scatter(lax.dot_general(tokens, cotangent, (((0,), (0,)), ((), (...  298 us
    all_gather x1, waiting for transfers between devices, on_device(): lax.all_gather(weight_half, 'fsdp', axis=0, tiled=True)  122 us
    all_gather x1, blocking collectives, on_device(): gathered = lax.all_gather(flat_sent, 'rep', axis=0, tiled=True)  44.2 us
  transfers between devices with their start and end apart: 2, of which 2 were waited for; matrix products, arithmetic and copies ran while one was open for 1% of the time, Pallas kernels for 0%

commit v1 on v0

v1 whole, which is shorter than its diff:
```python
import math

import jax
import jax.numpy as jnp
import numpy as np
from jax import lax
from jax.experimental import pallas as pl
from jax.experimental.pallas import tpu as pltpu
from jax.sharding import PartitionSpec as P

KW = 256
BLOCK = 64
SEL = 16
NX, NYH, NY, NZ = 8, 2, 4, 8
GROUP_TOK = 12288
MOMENTUM_DECAY = 0.9
LEARN_RATE = 0.05
MESH = pl.DeviceIdType.MESH
F32 = jnp.float32
BF16 = jnp.bfloat16
HI = lax.Precision.HIGHEST

UP = (2, 1)
DOWN = (3, 0)


def dct_rows():
    n = np.arange(BLOCK, dtype=np.float64)
    table = np.cos(math.pi * (2.0 * n[None, :] + 1.0) * n[:, None] / (2.0 * BLOCK)) * math.sqrt(2.0 / BLOCK)
    table[0] *= math.sqrt(0.5)
    return np.tile(table.T, (KW // BLOCK, 1)).astype(np.float32)


def make_slots():
    slots = {}

    def slot(*key):
        if key not in slots:
            slots[key] = len(slots)
        return slots[key]

    return slot


N_SLOTS = 112


def body(
    order, tok, cot, weight, mom, dct,
    ig, nm, up, nw,
    wf, own, psend, precv, rsend, rrecv, ysend, yrecv, c1s, c1r, c2r,
    ss, rs,
):
    slot = make_slots()
    rep = lax.axis_index("rep")
    mem = lax.axis_index("fsdp")
    x, yh = rep // 2, rep % 2
    y, z, core = mem // 16, (mem // 2) % 8, mem % 2

    def dev(x_, yh_, y_, z_, core_):
        return (x_ * 2 + yh_, y_ * 16 + z_ * 2 + core_)

    def at_z(d):
        return dev(x, yh, y, lax.rem(z + d, NZ), core)

    def at_y(e):
        return dev(x, yh, lax.rem(y + e, NY), z, core)

    def at_ring_y(d):
        full = lax.rem(yh * NY + y + d, NY * NYH)
        return dev(x, full // NY, full % NY, z, core)

    def at_x(d):
        return dev(lax.rem(x + d, NX), yh, y, z, core)

    sibling = dev(x, yh, y, z, 1 - core)
    mirror = dev(x, 1 - yh, y, z, core)

    partners = [sibling, mirror]
    partners += [at_z(d) for d in range(1, NZ)]
    partners += [at_x(d) for d in range(1, NX)]
    partners += [at_y(e) for e in range(1, NY)]
    partners += [at_ring_y(d) for d in (1, 2, 6, 7)]
    barrier = pltpu.get_barrier_semaphore()
    for p in partners:
        pl.semaphore_signal(barrier, inc=1, device_id=p, device_id_type=MESH)

    started = []

    def copy(key, src, dst, device):
        i = slot(*key)
        return pltpu.make_async_remote_copy(
            src_ref=src, dst_ref=dst, send_sem=ss.at[i], recv_sem=rs.at[i],
            device_id=device, device_id_type=MESH,
        )

    def send(key, src, dst, device):
        c = copy(key, src, dst, device)
        c.start()
        started.append(c)

    def arrived(key, dst):
        copy(key, dst, dst, sibling).wait_recv()

    chip = y * NZ + z

    def piece(x_):
        return x_ % 2, x_ // 2

    half, rb = piece(x)
    wf[half, chip, core, rb] = weight[
        pl.ds(pl.multiple_of(rb * 16, 16), 16), pl.ds(pl.multiple_of(half * 128, 128), 128)
    ].astype(BF16)

    pl.semaphore_wait(barrier, len(partners))

    own_piece = wf.at[half, chip, core, rb]
    for d in range(1, NZ):
        send(("gz", d), own_piece, own_piece, at_z(d))

    def partial(d):
        for e in range(NY):
            target = lax.rem(y + e, NY) * NZ + lax.rem(z + d, NZ)
            both = lax.dot_general(
                tok[:, pl.ds(pl.multiple_of(target * 128, 128), 128)], cot[...],
                (((0,), (0,)), ((), ())), preferred_element_type=F32,
            )
            low, high = both[:64], both[64:]
            own[d, e] = jnp.where(core == 0, low, high)
            psend[d, e] = jnp.where(core == 0, high, low).astype(BF16)
        send(("pair", d), psend.at[d], precv.at[d], sibling)

    for d in (4, 3, 5, 2, 6, 1, 7, 0):
        partial(d)

    def hop(h, direction, e):
        d = 4 - h if direction == 0 else 4 + h
        total = own[d, e] + precv[d, e].astype(F32)
        first = UP if direction == 0 else DOWN
        if h > 1 or (h == 1 and e in first):
            arrived(("ring", direction, h - 1, e), rrecv.at[direction, h - 1, e])
            total = total + rrecv[direction, h - 1, e].astype(F32)
        rsend[direction, h, e] = total.astype(BF16)
        send(
            ("ring", direction, h, e), rsend.at[direction, h, e], rrecv.at[direction, h, e],
            at_z(1 if direction == 0 else 7),
        )

    arrived(("pair", 4), precv.at[4])
    for i in range(2):
        hop(0, 0, UP[i])
        hop(0, 1, DOWN[i])
    arrived(("pair", 3), precv.at[3])
    arrived(("pair", 5), precv.at[5])
    for i in range(2):
        hop(1, 0, DOWN[i])
        hop(1, 1, UP[i])

    for d in range(1, NZ):
        arrived(("gz", d), own_piece)
    y_block = wf.at[half, pl.ds(y * NZ, NZ), core, rb]
    for d in (1, 7, 2):
        send(("gy", d), y_block, y_block, at_ring_y(d))

    for i in range(2):
        hop(1, 0, UP[i])
        hop(1, 1, DOWN[i])

    for d in (1, 7, 2):
        arrived(("gy", d), y_block)

    def x_part(x_, part):
        h_, r_ = piece(x_)
        return wf.at[h_, pl.ds(part * 16, 16), core, r_]

    def x_all(x_):
        h_, r_ = piece(x_)
        return wf.at[h_, :, core, r_]

    def gather_x(h, direction):
        origin = lax.rem(x + (NX - h if direction == 0 else h), NX)
        parts = (0, 1) if h < 3 else (direction,)
        for part in (0, 1):
            ref = x_part(origin, part)
            if h > 0:
                arrived(("gx", direction, h - 1, part), ref)
            if part in parts:
                send(("gx", direction, h, part), ref, ref, at_x(1 if direction == 0 else 7))
        if h > 0:
            send(("gc", direction, h), x_all(origin), x_all(origin), sibling)

    for direction in (0, 1):
        gather_x(0, direction)
    send(("gc", 0, 0), x_all(x), x_all(x), sibling)

    arrived(("pair", 2), precv.at[2])
    arrived(("pair", 6), precv.at[6])
    for i in range(2):
        hop(2, 0, DOWN[i])
        hop(2, 1, UP[i])
    for i in range(2):
        hop(2, 0, UP[i])
        hop(2, 1, DOWN[i])

    row = lax.broadcasted_iota(jnp.int32, (BLOCK, 128), 0)
    lane = lax.broadcasted_iota(jnp.int32, (BLOCK, 128), 1)
    picked = jnp.zeros((BLOCK, 128), F32)
    for s in range(SEL):
        picked = jnp.where((lane % SEL == s) & (row == order[s]), 1.0, picked)
    wide = lax.dot_general(dct[...], picked, (((1,), (0,)), ((), ())), precision=HI, preferred_element_type=F32)
    row_block = lax.broadcasted_iota(jnp.int32, (KW, 128), 0) // BLOCK
    lane_block = lax.broadcasted_iota(jnp.int32, (KW, 128), 1) // SEL
    basis0 = jnp.where(row_block == lane_block, wide, 0.0)
    basis1 = jnp.where(row_block + 4 == lane_block, wide, 0.0)

    gather_x(1, 0)
    gather_x(1, 1)

    arrived(("pair", 1), precv.at[1])
    arrived(("pair", 7), precv.at[7])
    for i in range(2):
        hop(3, 0, DOWN[i])
        hop(3, 1, UP[i])
    for i in range(2):
        hop(3, 0, UP[i])
        hop(3, 1, DOWN[i])

    gather_x(2, 0)
    gather_x(2, 1)

    arrived(("pair", 0), precv.at[0])

    def z_total(e):
        total = own[0, e] + precv[0, e].astype(F32)
        for direction in (0, 1):
            arrived(("ring", direction, 3, e), rrecv.at[direction, 3, e])
            total = total + rrecv[direction, 3, e].astype(F32)
        return total

    for e in (2, 3, 1):
        ysend[e] = z_total(e).astype(BF16)
        send(("y", e), ysend.at[e], yrecv.at[e], at_y(e))
    grad = z_total(0)

    gather_x(3, 0)
    gather_x(3, 1)

    for e in (1, 3, 2):
        arrived(("y", e), yrecv.at[e])
        grad = grad + yrecv[e].astype(F32)

    moment = MOMENTUM_DECAY * mom[0] + grad * (float(GROUP_TOK) ** -0.5)
    compact = lax.dot_general(
        moment[:32], basis0, (((1,), (0,)), ((), ())), precision=HI, preferred_element_type=F32
    ) + lax.dot_general(
        moment[32:], basis1, (((1,), (0,)), ((), ())), precision=HI, preferred_element_type=F32
    )
    c1s[...] = compact
    send(("mirror",), c1s, c1r, mirror)

    nm[0, :32] = moment[:32] - lax.dot_general(
        compact, basis0, (((1,), (1,)), ((), ())), precision=HI, preferred_element_type=F32
    )
    nm[0, 32:] = moment[32:] - lax.dot_general(
        compact, basis1, (((1,), (1,)), ((), ())), precision=HI, preferred_element_type=F32
    )

    arrived(("mirror",), c1r)
    c2r[x] = (compact + c1r[...]).astype(BF16)
    for d in range(1, NX):
        send(("rep", d), c2r.at[x], c2r.at[x], at_x(d))

    far = lax.rem(x + 4, NX)
    arrived(("gx", 0, 3, 0), x_part(far, 0))
    arrived(("gx", 1, 3, 1), x_part(far, 1))
    send(("gc", 0, 4), x_all(far), x_all(far), sibling)
    for key in [("gc", 0, h) for h in range(5)] + [("gc", 1, h) for h in range(1, 4)]:
        arrived(key, x_all(x))

    for i in range(8):
        w = jnp.concatenate(
            [wf[k, 4 * i:4 * i + 4].reshape(512, 128) for k in range(2)], axis=1
        )
        ig[:, 512 * i:512 * i + 512] = lax.dot_general(
            cot[...], w, (((1,), (1,)), ((), ())), preferred_element_type=F32
        ).astype(BF16)

    for d in range(1, NX):
        arrived(("rep", d), c2r.at[0])
    total = c2r[0].astype(F32)
    for i in range(1, NX):
        total = total + c2r[i].astype(F32)
    total = total * (1.0 / (NX * NYH))
    for i, basis in enumerate((basis0, basis1)):
        rows = slice(32 * i, 32 * i + 32)
        update = lax.dot_general(total, basis, (((1,), (1,)), ((), ())), precision=HI, preferred_element_type=F32)
        up[rows] = update
        nw[rows] = weight[rows] - LEARN_RATE * update

    for c in started:
        c.wait_send()


def on_device(tokens, cotangent, weight, momentum, column_order):
    vmem = pl.BlockSpec(memory_space=pltpu.VMEM)
    smem = pl.BlockSpec(memory_space=pltpu.SMEM)
    return pl.pallas_call(
        body,
        out_shape=(
            jax.ShapeDtypeStruct((tokens.shape[0], tokens.shape[1]), BF16),
            jax.ShapeDtypeStruct(momentum.shape, F32),
            jax.ShapeDtypeStruct(weight.shape, F32),
            jax.ShapeDtypeStruct(weight.shape, F32),
        ),
        in_specs=[smem, vmem, vmem, vmem, vmem, vmem],
        out_specs=(vmem, vmem, vmem, vmem),
        scratch_shapes=[
            pltpu.VMEM((2, NY * NZ, 2, 4, 16, 128), BF16),
            pltpu.VMEM((NZ, NY, 64, KW), F32),
            pltpu.VMEM((NZ, NY, 64, KW), BF16),
            pltpu.VMEM((NZ, NY, 64, KW), BF16),
            pltpu.VMEM((2, 4, NY, 64, KW), BF16),
            pltpu.VMEM((2, 4, NY, 64, KW), BF16),
            pltpu.VMEM((NY, 64, KW), BF16),
            pltpu.VMEM((NY, 64, KW), BF16),
            pltpu.VMEM((32, 128), F32),
            pltpu.VMEM((32, 128), F32),
            pltpu.VMEM((NX, 32, 128), BF16),
            pltpu.SemaphoreType.DMA((N_SLOTS,)),
            pltpu.SemaphoreType.DMA((N_SLOTS,)),
        ],
        compiler_params=pltpu.CompilerParams(
            collective_id=0, has_side_effects=True, vmem_limit_bytes=40 * 1024 * 1024
        ),
        name="demo_step",
    )(column_order, tokens, cotangent, weight, momentum, jnp.asarray(dct_rows()))


def solution(mesh):
    in_specs = (
        P(("rep", "fsdp"), None),
        P(("rep", "fsdp"), None),
        P("fsdp", None),
        P("rep", "fsdp", None),
        P(),
    )
    out_specs = (P(("rep", "fsdp"), None), P("rep", "fsdp", None), P("fsdp", None), P("fsdp", None))
    return jax.shard_map(
        on_device, mesh=mesh, in_specs=in_specs, out_specs=out_specs, check_vma=False
    )
```

time: 496 us -> 67.5 us (0.14)
  the two profiles are of different devices: /device:TPU:1 before, /device:TPU:14 now
where the time goes in v1:
time: 67.5 us; the launch traced here: 67.2 us
  Pallas kernels  58 us (86%)
  local copies, waits for them, and re-layouts  8.56 us (13%)
    pallas_call x1, Pallas kernels, on_device(): pl.pallas_call(body, out_shape=(jax.ShapeDtypeStruct((tokens.shape[0], to...  58 us
    unnamed x16, local copies, waits for them, and re-layouts  8.56 us

profile of v1, /device:TPU:14, one launch (start us, length us, event | category | flops | bytes accessed | tf_op | source)
XLA Modules:
  0.0 67.2 jit_solution(16879796580165974591)
XLA Ops:
  0.6 0.0 copy-start
  0.6 1.4 %copy-done = bf16[192,4096]{1,0:T(8,128)(2,1)S(1)} copy-done((bf16[192,4096]{1,0:T(8,128)(2,1)S(1)}, bf16[192,4096]{1,0:T(8,128)(2,1)}, u32[]{:S(2)}) %copy-start) | copy-done | bytes 1572888
  2.0 0.0 copy-start.1
  2.0 0.9 %copy-done.1 = f32[256,64]{1,0:T(8,128)S(1)} copy-done((f32[256,64]{1,0:T(8,128)S(1)}, f32[256,64]{1,0:T(8,128)}, u32[]{:S(2)}) %copy-start.1) | copy-done | bytes 65560
  2.9 0.0 copy-start.2
  2.9 0.9 %copy-done.2 = bf16[192,256]{1,0:T(8,128)(2,1)S(1)} copy-done((bf16[192,256]{1,0:T(8,128)(2,1)S(1)}, bf16[192,256]{1,0:T(8,128)(2,1)}, u32[]{:S(2)}) %copy-start.2) | copy-done | bytes 98328
  3.8 0.0 copy-start.3
  3.8 0.8 %copy-done.3 = f32[64,256]{1,0:T(8,128)S(1)} copy-done((f32[64,256]{1,0:T(8,128)S(1)}, f32[64,256]{1,0:T(8,128)}, u32[]{:S(2)}) %copy-start.3) | copy-done | bytes 65560
  4.7 0.0 copy-start.4
  4.7 0.8 %copy-done.4 = f32[1,64,256]{2,1,0:T(8,128)S(1)} copy-done((f32[1,64,256]{2,1,0:T(8,128)S(1)}, f32[1,64,256]{2,1,0:T(8,128)}, u32[]{:S(2)}) %copy-start.4) | copy-done | bytes 65560
  5.5 0.0 copy-start.5
  5.5 0.7 copy-done.5
  6.2 58.0 %demo_step.1 = (bf16[192,4096]{1,0:T(8,128)(2,1)S(1)}, f32[1,64,256]{2,1,0:T(8,128)S(1)}, f32[64,256]{1,0:T(8,128)S(1)}, f32[64,256]{1,0:T(8,128)S(1)}) custom-call(s32[64]{0:T(128)S(1)} %copy-done.5, bf16[192,4096]{1,0:T(8,128)(2,1)S(1)} %copy-done, bf16[192,256]{1,0:T(8,128)(2,1)S(1)} %copy-done.2, f32[64,256]{1,0:T(8,128)S(1)} %copy-done.3, ...), custom_call_target="tpu_custom_call" | custom-call | tf_op jit(solution)/shard_map/demo_step/pallas_call | solution.py:307
  64.2 1.1 %copy.14 = bf16[192,4096]{1,0:T(8,128)(2,1)} copy(bf16[192,4096]{1,0:T(8,128)(2,1)S(1)} %get-tuple-element.8) | data formatting | bytes 3145728
  65.3 0.6 copy.15
  65.9 0.6 copy.16
  66.6 0.6 copy.17
Async XLA Ops:
  0.6 1.4 %copy-start = (bf16[192,4096]{1,0:T(8,128)(2,1)S(1)}, bf16[192,4096]{1,0:T(8,128)(2,1)}, u32[]{:S(2)}) copy-start(bf16[192,4096]{1,0:T(8,128)(2,1)} %tok.1) | copy-start | bytes 4718596
  2.0 0.9 %copy-start.1 = (f32[256,64]{1,0:T(8,128)S(1)}, f32[256,64]{1,0:T(8,128)}, u32[]{:S(2)}) copy-start(f32[256,64]{1,0:T(8,128)} %constant.2.clone.dct) | copy-start | bytes 196612
  2.9 0.9 %copy-start.2 = (bf16[192,256]{1,0:T(8,128)(2,1)S(1)}, bf16[192,256]{1,0:T(8,128)(2,1)}, u32[]{:S(2)}) copy-start(bf16[192,256]{1,0:T(8,128)(2,1)} %cot.1) | copy-start | bytes 294916
  3.8 0.8 %copy-start.3 = (f32[64,256]{1,0:T(8,128)S(1)}, f32[64,256]{1,0:T(8,128)}, u32[]{:S(2)}) copy-start(f32[64,256]{1,0:T(8,128)} %weight.1) | copy-start | bytes 196612
  4.7 0.8 %copy-start.4 = (f32[1,64,256]{2,1,0:T(8,128)S(1)}, f32[1,64,256]{2,1,0:T(8,128)}, u32[]{:S(2)}) copy-start(f32[1,64,256]{2,1,0:T(8,128)} %mom.1) | copy-start | bytes 196612
  5.5 0.7 copy-start.5

commit v2 on v1

v2 whole, which is shorter than its diff:
```python
import math

import jax
import jax.numpy as jnp
import numpy as np
from jax import lax
from jax.experimental import pallas as pl
from jax.experimental.pallas import tpu as pltpu
from jax.sharding import PartitionSpec as P

KW = 256
BLOCK = 64
SEL = 16
NX, NYH, NY, NZ = 8, 2, 4, 8
GROUP_TOK = 12288
MOMENTUM_DECAY = 0.9
LEARN_RATE = 0.05
MESH = pl.DeviceIdType.MESH
F32 = jnp.float32
BF16 = jnp.bfloat16
HI = lax.Precision.HIGHEST

UP = (2, 1)
DOWN = (3, 0)
LATE = (2, 3, 1, 0)

PARTS = (0, 1, 3, 2)
LAST = ((0, 3), (1, 2))


def dct_rows():
    n = np.arange(BLOCK, dtype=np.float64)
    table = np.cos(math.pi * (2.0 * n[None, :] + 1.0) * n[:, None] / (2.0 * BLOCK)) * math.sqrt(2.0 / BLOCK)
    table[0] *= math.sqrt(0.5)
    return np.tile(table.T, (KW // BLOCK, 1)).astype(np.float32)


def make_slots():
    slots = {}

    def slot(*key):
        if key not in slots:
            slots[key] = len(slots)
        return slots[key]

    return slot


N_SLOTS = 128


def body(
    order_hbm, tok_hbm, cot_hbm, weight_hbm, mom_hbm, dct_hbm,
    ig_hbm, nm_hbm, up_hbm, nw_hbm,
    ig, nm, up, nw,
    order, tok, cot, weight, mom, dct,
    wf, own, psend, precv, rsend, rrecv, ysend, yrecv, csend, crecv, cmom, c2r,
    ss, rs, ls,
):
    slot = make_slots()
    local = [
        pltpu.make_async_copy(src, dst, ls.at[i])
        for i, (src, dst) in enumerate((
            (weight_hbm, weight), (cot_hbm, cot), (tok_hbm, tok), (mom_hbm, mom), (dct_hbm, dct), (order_hbm, order),
        ))
    ]
    for c in local:
        c.start()
    rep = lax.axis_index("rep")
    mem = lax.axis_index("fsdp")
    x, yh = rep // 2, rep % 2
    y, z, core = mem // 16, (mem // 2) % 8, mem % 2

    def dev(x_, yh_, y_, z_, core_):
        return (x_ * 2 + yh_, y_ * 16 + z_ * 2 + core_)

    def at_z(d):
        return dev(x, yh, y, lax.rem(z + d, NZ), core)

    def at_y(e):
        return dev(x, yh, lax.rem(y + e, NY), z, core)

    def across(e):
        return dev(x, 1 - yh, lax.rem(y + e, NY), z, core)

    def at_ring_y(d):
        full = lax.rem(yh * NY + y + d, NY * NYH)
        return dev(x, full // NY, full % NY, z, core)

    def at_x(d):
        return dev(lax.rem(x + d, NX), yh, y, z, core)

    sibling = dev(x, yh, y, z, 1 - core)

    partners = [sibling, across(0)]
    partners += [at_z(d) for d in range(1, NZ)]
    partners += [at_x(d) for d in range(1, NX)]
    partners += [at_y(e) for e in range(1, NY)]
    partners += [at_ring_y(d) for d in (1, 2, 6, 7)]
    partners += [across(e) for e in range(1, NY)]
    barrier = pltpu.get_barrier_semaphore()
    for p in partners:
        pl.semaphore_signal(barrier, inc=1, device_id=p, device_id_type=MESH)

    started = []
    stores = []

    def store(i, src, dst):
        c = pltpu.make_async_copy(src, dst, ls.at[i])
        c.start()
        stores.append(c)

    def copy(key, src, dst, device):
        i = slot(*key)
        return pltpu.make_async_remote_copy(
            src_ref=src, dst_ref=dst, send_sem=ss.at[i], recv_sem=rs.at[i],
            device_id=device, device_id_type=MESH,
        )

    def send(key, src, dst, device):
        c = copy(key, src, dst, device)
        c.start()
        started.append(c)

    def arrived(key, dst):
        copy(key, dst, dst, sibling).wait_recv()

    def partial(d):
        for e in range(NY):
            target = lax.rem(y + e, NY) * NZ + lax.rem(z + d, NZ)
            both = lax.dot_general(
                tok[:, pl.ds(pl.multiple_of(target * 128, 128), 128)], cot[...],
                (((0,), (0,)), ((), ())), preferred_element_type=F32,
            )
            low, high = both[:64], both[64:]
            own[d, e] = jnp.where(core == 0, low, high)
            psend[d, e] = jnp.where(core == 0, high, low).astype(BF16)

    def pair(d):
        send(("pair", d), psend.at[d], precv.at[d], sibling)

    chip = y * NZ + z

    def piece(x_):
        return x_ % 2, x_ // 2

    half, rb = piece(x)
    local[0].wait()
    wf[half, chip, core, rb] = weight[
        pl.ds(pl.multiple_of(rb * 16, 16), 16), pl.ds(pl.multiple_of(half * 128, 128), 128)
    ].astype(BF16)
    own_piece = wf.at[half, chip, core, rb]

    local[1].wait()
    local[2].wait()
    for d in (4, 3, 5):
        partial(d)

    pl.semaphore_wait(barrier, len(partners))

    for d in (4, 3, 5):
        pair(d)
    for d in range(1, NZ):
        send(("gz", d), own_piece, own_piece, at_z(d))

    def hop(h, direction, e):
        d = 4 - h if direction == 0 else 4 + h
        total = own[d, e] + precv[d, e].astype(F32)
        first = UP if direction == 0 else DOWN
        if h > 1 or (h == 1 and e in first):
            arrived(("ring", direction, h - 1, e), rrecv.at[direction, h - 1, e])
            total = total + rrecv[direction, h - 1, e].astype(F32)
        rsend[direction, h, e] = total.astype(BF16)
        send(
            ("ring", direction, h, e), rsend.at[direction, h, e], rrecv.at[direction, h, e],
            at_z(1 if direction == 0 else 7),
        )

    def x_part(x_, e):
        h_, r_ = piece(x_)
        return wf.at[h_, pl.ds(lax.rem(y + e, NY) * NZ, NZ), core, r_]

    def x_all(x_):
        h_, r_ = piece(x_)
        return wf.at[h_, :, core, r_]

    def origin(h, direction):
        return lax.rem(x + (NX - h if direction == 0 else h), NX)

    def gather_x(h, direction, e):
        ref = x_part(origin(h, direction), e)
        if h > 0:
            arrived(("gx", direction, h - 1, e), ref)
        if h < 3 or e in LAST[direction]:
            send(("gx", direction, h, e), ref, ref, at_x(1 if direction == 0 else 7))

    def gather_core(h, direction):
        ref = x_all(origin(h, direction))
        send(("gc", direction, h), ref, ref, sibling)

    for d in (2, 6):
        partial(d)
        pair(d)
    arrived(("pair", 4), precv.at[4])
    for i in range(2):
        hop(0, 0, UP[i])
        hop(0, 1, DOWN[i])
    for d in (1, 7, 0):
        partial(d)
        pair(d)
    arrived(("pair", 3), precv.at[3])
    arrived(("pair", 5), precv.at[5])
    for i in range(2):
        hop(1, 0, DOWN[i])
        hop(1, 1, UP[i])

    for i in range(2):
        hop(1, 0, UP[i])
        hop(1, 1, DOWN[i])

    for d in range(1, NZ):
        arrived(("gz", d), own_piece)
    y_block = x_part(x, 0)
    for d in (1, 7, 2):
        send(("gy", d), y_block, y_block, at_ring_y(d))
    for direction in (0, 1):
        gather_x(0, direction, 0)

    for i in (3, 4, 5):
        local[i].wait()

    row = lax.broadcasted_iota(jnp.int32, (BLOCK, 128), 0)
    lane = lax.broadcasted_iota(jnp.int32, (BLOCK, 128), 1)
    picked = jnp.zeros((BLOCK, 128), F32)
    for s in range(SEL):
        picked = jnp.where((lane % SEL == s) & (row == order[s]), 1.0, picked)
    wide = lax.dot_general(dct[...], picked, (((1,), (0,)), ((), ())), precision=HI, preferred_element_type=F32)
    row_block = lax.broadcasted_iota(jnp.int32, (KW, 128), 0) // BLOCK
    lane_block = lax.broadcasted_iota(jnp.int32, (KW, 128), 1) // SEL
    basis0 = jnp.where(row_block == lane_block, wide, 0.0)
    basis1 = jnp.where(row_block + 4 == lane_block, wide, 0.0)

    def project(upper, lower):
        return lax.dot_general(
            upper, basis0, (((1,), (0,)), ((), ())), precision=HI, preferred_element_type=F32
        ) + lax.dot_general(
            lower, basis1, (((1,), (0,)), ((), ())), precision=HI, preferred_element_type=F32
        )

    decayed = MOMENTUM_DECAY * mom[0]
    cmom[yh] = project(decayed[:32], decayed[32:])
    send(("old",), cmom.at[yh], cmom.at[yh], across(0))

    arrived(("pair", 2), precv.at[2])
    arrived(("pair", 6), precv.at[6])
    for e in LATE:
        hop(2, 0, e)
        hop(2, 1, e)

    for d, e in ((7, 1), (1, 3), (2, 2)):
        arrived(("gy", d), x_part(x, e))
        for direction in (0, 1):
            gather_x(0, direction, e)
    gather_core(0, 0)

    arrived(("pair", 1), precv.at[1])
    arrived(("pair", 7), precv.at[7])
    for e in LATE:
        hop(3, 0, e)
        hop(3, 1, e)

    def gather_step(h):
        for e in PARTS:
            gather_x(h, 0, e)
            gather_x(h, 1, e)
        gather_core(h, 0)
        gather_core(h, 1)

    gather_step(1)

    arrived(("pair", 0), precv.at[0])

    def z_total(e):
        total = own[0, e] + precv[0, e].astype(F32)
        for direction in (0, 1):
            arrived(("ring", direction, 3, e), rrecv.at[direction, 3, e])
            total = total + rrecv[direction, 3, e].astype(F32)
        return total

    place = yh * NY + y
    for both in (LATE[:2], LATE[2:]):
        sums = [z_total(e) for e in both]
        columns = project(
            jnp.concatenate([t[:32] for t in sums], axis=0), jnp.concatenate([t[32:] for t in sums], axis=0)
        ).astype(BF16)
        for i, e in enumerate(both):
            csend[e] = columns[32 * i:32 * i + 32]
            send(("across", e), csend.at[e], crecv.at[place], across(e))
            if e > 0:
                send(("along", e), csend.at[e], crecv.at[place], at_y(e))
            else:
                crecv[place] = columns[32 * i:32 * i + 32]
        for i, e in enumerate(both):
            if e > 0:
                ysend[e] = sums[i].astype(BF16)
                send(("y", e), ysend.at[e], yrecv.at[e], at_y(e))
            else:
                grad = sums[i]

    gather_step(2)

    scale = float(GROUP_TOK) ** -0.5
    arrived(("old",), cmom.at[0])
    for e in LATE[:3]:
        arrived(("along", e), crecv.at[0])
    for e in LATE:
        arrived(("across", e), crecv.at[0])
    shared = crecv[0].astype(F32)
    for i in range(1, NYH * NY):
        shared = shared + crecv[i].astype(F32)
    c2r[x] = (shared * scale + (cmom[0] + cmom[1])).astype(BF16)
    for d in (4, 3, 5, 2, 6, 1, 7):
        send(("rep", d), c2r.at[x], c2r.at[x], at_x(d))

    gather_step(3)

    for e in LATE[:3]:
        arrived(("y", e), yrecv.at[e])
        grad = grad + yrecv[e].astype(F32)
    moment = decayed + grad * scale
    compact = project(moment[:32], moment[32:])
    nm[0, :32] = moment[:32] - lax.dot_general(
        compact, basis0, (((1,), (1,)), ((), ())), precision=HI, preferred_element_type=F32
    )
    nm[0, 32:] = moment[32:] - lax.dot_general(
        compact, basis1, (((1,), (1,)), ((), ())), precision=HI, preferred_element_type=F32
    )
    store(6, nm, nm_hbm)

    far = lax.rem(x + 4, NX)
    for direction in (0, 1):
        for e in LAST[direction]:
            arrived(("gx", direction, 3, e), x_part(far, e))
    send(("gc", 0, 4), x_all(far), x_all(far), sibling)
    for key in [("gc", 0, h) for h in range(5)] + [("gc", 1, h) for h in range(1, 4)]:
        arrived(key, x_all(x))

    for i in range(8):
        w = jnp.concatenate(
            [wf[k, 4 * i:4 * i + 4].reshape(512, 128) for k in range(2)], axis=1
        )
        ig[:, 512 * i:512 * i + 512] = lax.dot_general(
            cot[...], w, (((1,), (1,)), ((), ())), preferred_element_type=F32
        ).astype(BF16)
    store(7, ig, ig_hbm)

    for d in range(1, NX):
        arrived(("rep", d), c2r.at[0])
    total = c2r[0].astype(F32)
    for i in range(1, NX):
        total = total + c2r[i].astype(F32)
    total = total * (1.0 / (NX * NYH))
    for i, basis in enumerate((basis0, basis1)):
        rows = slice(32 * i, 32 * i + 32)
        update = lax.dot_general(total, basis, (((1,), (1,)), ((), ())), precision=HI, preferred_element_type=F32)
        up[rows] = update
        nw[rows] = weight[rows] - LEARN_RATE * update

    store(8, up, up_hbm)
    store(9, nw, nw_hbm)
    for c in started:
        c.wait_send()
    for c in stores:
        c.wait()


def finish(ig, nm, up, nw, ig_out, nm_out, up_out, nw_out, ig_v, nm_v, up_v, nw_v, sems):
    moves = [(nm, nm_v, nm_out), (up, up_v, up_out), (nw, nw_v, nw_out)]
    rows = ig.shape[0] // 4
    moves += [tuple(r.at[rows * i:rows * i + rows] for r in (ig, ig_v, ig_out)) for i in range(4)]
    loads = [pltpu.make_async_copy(src, mid, sems.at[0, i]) for i, (src, mid, _) in enumerate(moves)]
    stores = [pltpu.make_async_copy(mid, dst, sems.at[1, i]) for i, (_, mid, dst) in enumerate(moves)]
    for c in loads:
        c.start()
    for load, store in zip(loads, stores):
        load.wait()
        store.start()
    for c in stores:
        c.wait()


def on_device(tokens, cotangent, weight, momentum, column_order):
    hbm = pl.BlockSpec(memory_space=pltpu.HBM)
    shapes = (
        jax.ShapeDtypeStruct(tokens.shape, BF16),
        jax.ShapeDtypeStruct(momentum.shape, F32),
        jax.ShapeDtypeStruct(weight.shape, F32),
        jax.ShapeDtypeStruct(weight.shape, F32),
    )
    table = jnp.asarray(dct_rows())
    results = pl.pallas_call(
        body,
        out_shape=shapes,
        in_specs=[hbm] * 6,
        out_specs=(hbm,) * 4,
        scratch_shapes=[pltpu.VMEM(a.shape, a.dtype) for a in shapes] + [
            pltpu.SMEM(column_order.shape, jnp.int32),
            pltpu.VMEM(tokens.shape, BF16),
            pltpu.VMEM(cotangent.shape, BF16),
            pltpu.VMEM(weight.shape, F32),
            pltpu.VMEM(momentum.shape, F32),
            pltpu.VMEM(table.shape, F32),
            pltpu.VMEM((2, NY * NZ, 2, 4, 16, 128), BF16),
            pltpu.VMEM((NZ, NY, 64, KW), F32),
            pltpu.VMEM((NZ, NY, 64, KW), BF16),
            pltpu.VMEM((NZ, NY, 64, KW), BF16),
            pltpu.VMEM((2, 4, NY, 64, KW), BF16),
            pltpu.VMEM((2, 4, NY, 64, KW), BF16),
            pltpu.VMEM((NY, 64, KW), BF16),
            pltpu.VMEM((NY, 64, KW), BF16),
            pltpu.VMEM((NY, 32, 128), BF16),
            pltpu.VMEM((NYH * NY, 32, 128), BF16),
            pltpu.VMEM((NYH, 32, 128), F32),
            pltpu.VMEM((NX, 32, 128), BF16),
            pltpu.SemaphoreType.DMA((N_SLOTS,)),
            pltpu.SemaphoreType.DMA((N_SLOTS,)),
            pltpu.SemaphoreType.DMA((10,)),
        ],
        compiler_params=pltpu.CompilerParams(
            collective_id=0, has_side_effects=True, vmem_limit_bytes=57 * 1024 * 1024
        ),
        name="demo_step",
    )(column_order, tokens, cotangent, weight, momentum, table)
    return pl.pallas_call(
        finish,
        out_shape=shapes,
        in_specs=[hbm] * 4,
        out_specs=(hbm,) * 4,
        scratch_shapes=[pltpu.VMEM(a.shape, a.dtype) for a in shapes] + [pltpu.SemaphoreType.DMA((2, 7))],
        compiler_params=pltpu.CompilerParams(vmem_limit_bytes=57 * 1024 * 1024),
        name="store_results",
    )(*results)


def solution(mesh):
    in_specs = (
        P(("rep", "fsdp"), None),
        P(("rep", "fsdp"), None),
        P("fsdp", None),
        P("rep", "fsdp", None),
        P(),
    )
    out_specs = (P(("rep", "fsdp"), None), P("rep", "fsdp", None), P("fsdp", None), P("fsdp", None))
    return jax.shard_map(
        on_device, mesh=mesh, in_specs=in_specs, out_specs=out_specs, check_vma=False
    )
```

time: 67.5 us -> 58 us (0.86)
  the two profiles are of different devices: /device:TPU:14 before, /device:TPU:1 now
where the time goes in v2:
time: 58 us; the launch traced here: 57.8 us
  Pallas kernels  57.1 us (98%)
  between operations  0.64 us (1%)
    pallas_call x1, Pallas kernels, on_device(): pl.pallas_call(body, out_shape=shapes, in_specs=[hbm] * 6, out_specs=(hbm...  54.8 us
    pallas_call x1, Pallas kernels, on_device(): pl.pallas_call(finish, out_shape=shapes, in_specs=[hbm] * 4, out_specs=(h...  2.36 us

profile of v2, /device:TPU:1, one launch (start us, length us, event | category | flops | bytes accessed | tf_op | source)
XLA Modules:
  0.0 57.8 jit_solution(1122268639994095920)
XLA Ops:
  0.6 54.8 %demo_step.1 = (bf16[192,4096]{1,0:T(8,128)(2,1)}, f32[1,64,256]{2,1,0:T(8,128)}, f32[64,256]{1,0:T(8,128)}, f32[64,256]{1,0:T(8,128)}) custom-call(s32[64]{0:T(128)} %order_hbm.1, bf16[192,4096]{1,0:T(8,128)(2,1)} %tok_hbm.1, bf16[192,256]{1,0:T(8,128)(2,1)} %cot_hbm.1, f32[64,256]{1,0:T(8,128)} %weight_hbm.1, f32[1,64,256]{2,1,0:T(8,128)} %mom_hbm.1, ...), custom_call_target="tpu_custom_call" | custom-call | tf_op jit(solution)/shard_map/demo_step/pallas_call | solution.py:401
  55.4 2.4 %store_results.1 = (bf16[192,4096]{1,0:T(8,128)(2,1)}, f32[1,64,256]{2,1,0:T(8,128)}, f32[64,256]{1,0:T(8,128)}, f32[64,256]{1,0:T(8,128)}) custom-call(bf16[192,4096]{1,0:T(8,128)(2,1)} %get-tuple-element.8.ig, f32[1,64,256]{2,1,0:T(8,128)} %get-tuple-element.9.nm, f32[64,256]{1,0:T(8,128)} %get-tuple-element.10.up, f32[64,256]{1,0:T(8,128)} %get-tuple-element.11.nw), custom_call_target="tpu_custom_call" | custom-call | tf_op jit(solution)/shard_map/store_results/pallas_call | solution.py:434

commit v3 on v2

--- a/solution.py
+++ b/solution.py
@@ -151,17 +151,16 @@
     ].astype(BF16)
     own_piece = wf.at[half, chip, core, rb]
 
+    pl.semaphore_wait(barrier, len(partners))
+
+    for d in (4, 3, 5, 2, 6, 1, 7):
+        send(("gz", d), own_piece, own_piece, at_z(d))
+
     local[1].wait()
     local[2].wait()
     for d in (4, 3, 5):
         partial(d)
-
-    pl.semaphore_wait(barrier, len(partners))
-
-    for d in (4, 3, 5):
         pair(d)
-    for d in range(1, NZ):
-        send(("gz", d), own_piece, own_piece, at_z(d))
 
     def hop(h, direction, e):
         d = 4 - h if direction == 0 else 4 + h
@@ -253,9 +252,9 @@
 
     arrived(("pair", 2), precv.at[2])
     arrived(("pair", 6), precv.at[6])
-    for e in LATE:
-        hop(2, 0, e)
-        hop(2, 1, e)
+    for up_e, down_e in zip(DOWN + UP, UP + DOWN):
+        hop(2, 0, up_e)
+        hop(2, 1, down_e)
 
     for d, e in ((7, 1), (1, 3), (2, 2)):
         arrived(("gy", d), x_part(x, e))
@@ -265,9 +264,9 @@
 
     arrived(("pair", 1), precv.at[1])
     arrived(("pair", 7), precv.at[7])
-    for e in LATE:
-        hop(3, 0, e)
-        hop(3, 1, e)
+    for up_e, down_e in zip(DOWN + UP, UP + DOWN):
+        hop(3, 0, up_e)
+        hop(3, 1, down_e)
 
     def gather_step(h):
         for e in PARTS:
@@ -288,6 +287,7 @@
         return total
 
     place = yh * NY + y
+    ysums = []
     for both in (LATE[:2], LATE[2:]):
         sums = [z_total(e) for e in both]
         columns = project(
@@ -300,12 +300,11 @@
                 send(("along", e), csend.at[e], crecv.at[place], at_y(e))
             else:
                 crecv[place] = columns[32 * i:32 * i + 32]
-        for i, e in enumerate(both):
-            if e > 0:
-                ysend[e] = sums[i].astype(BF16)
-                send(("y", e), ysend.at[e], yrecv.at[e], at_y(e))
-            else:
-                grad = sums[i]
+        ysums += zip(both, sums)
+    for e, total in ysums[:3]:
+        ysend[e] = total.astype(BF16)
+        send(("y", e), ysend.at[e], yrecv.at[e], at_y(e))
+    grad = ysums[3][1]
 
     gather_step(2)
 
@@ -337,6 +336,10 @@
     )
     store(6, nm, nm_hbm)
 
+    for c in started[:-15]:
+        c.wait_send()
+    del started[:-15]
+
     far = lax.rem(x + 4, NX)
     for direction in (0, 1):
         for e in LAST[direction]:
@@ -352,7 +355,9 @@
         ig[:, 512 * i:512 * i + 512] = lax.dot_general(
             cot[...], w, (((1,), (1,)), ((), ())), preferred_element_type=F32
         ).astype(BF16)
-    store(7, ig, ig_hbm)
+        if i % 2 == 1:
+            done = pl.ds(512 * (i - 1), 1024)
+            store(10 + i // 2, ig.at[:, done], ig_hbm.at[:, done])
 
     for d in range(1, NX):
         arrived(("rep", d), c2r.at[0])
@@ -424,7 +429,7 @@
             pltpu.VMEM((NX, 32, 128), BF16),
             pltpu.SemaphoreType.DMA((N_SLOTS,)),
             pltpu.SemaphoreType.DMA((N_SLOTS,)),
-            pltpu.SemaphoreType.DMA((10,)),
+            pltpu.SemaphoreType.DMA((14,)),
         ],
         compiler_params=pltpu.CompilerParams(
             collective_id=0, has_side_effects=True, vmem_limit_bytes=57 * 1024 * 1024

time: 58 us -> 57.3 us (0.988)
  Pallas kernels: 57.1 us -> 56.5 us
    pallas_call x1, Pallas kernels: 54.8 us -> 54.1 us  [on_device(): pl.pallas_call(body, out_shape=shapes, in_specs=[hbm] * 6, out_specs=(hbm...]
where the time goes in v3:
time: 57.3 us; the launch traced here: 57.1 us
  Pallas kernels  56.5 us (99%)
  between operations  0.64 us (1%)
    pallas_call x1, Pallas kernels, on_device(): pl.pallas_call(body, out_shape=shapes, in_specs=[hbm] * 6, out_specs=(hbm...  54.1 us
    pallas_call x1, Pallas kernels, on_device(): pl.pallas_call(finish, out_shape=shapes, in_specs=[hbm] * 4, out_specs=(h...  2.36 us

profile of v3, /device:TPU:1, one launch (start us, length us, event | category | flops | bytes accessed | tf_op | source)
XLA Modules:
  0.0 57.1 jit_solution(11868906544243249586)
XLA Ops:
  0.6 54.1 %demo_step.1 = (bf16[192,4096]{1,0:T(8,128)(2,1)}, f32[1,64,256]{2,1,0:T(8,128)}, f32[64,256]{1,0:T(8,128)}, f32[64,256]{1,0:T(8,128)}) custom-call(s32[64]{0:T(128)} %order_hbm.1, bf16[192,4096]{1,0:T(8,128)(2,1)} %tok_hbm.1, bf16[192,256]{1,0:T(8,128)(2,1)} %cot_hbm.1, f32[64,256]{1,0:T(8,128)} %weight_hbm.1, f32[1,64,256]{2,1,0:T(8,128)} %mom_hbm.1, ...), custom_call_target="tpu_custom_call" | custom-call | tf_op jit(solution)/shard_map/demo_step/pallas_call | solution.py:406
  54.8 2.4 %store_results.1 = (bf16[192,4096]{1,0:T(8,128)(2,1)}, f32[1,64,256]{2,1,0:T(8,128)}, f32[64,256]{1,0:T(8,128)}, f32[64,256]{1,0:T(8,128)}) custom-call(bf16[192,4096]{1,0:T(8,128)(2,1)} %get-tuple-element.8.ig, f32[1,64,256]{2,1,0:T(8,128)} %get-tuple-element.9.nm, f32[64,256]{1,0:T(8,128)} %get-tuple-element.10.up, f32[64,256]{1,0:T(8,128)} %get-tuple-element.11.nw), custom_call_target="tpu_custom_call" | custom-call | tf_op jit(solution)/shard_map/store_results/pallas_call | solution.py:439

commit v4 on v3

--- a/solution.py
+++ b/solution.py
@@ -186,12 +186,22 @@
     def origin(h, direction):
         return lax.rem(x + (NX - h if direction == 0 else h), NX)
 
-    def gather_x(h, direction, e):
-        ref = x_part(origin(h, direction), e)
-        if h > 0:
-            arrived(("gx", direction, h - 1, e), ref)
-        if h < 3 or e in LAST[direction]:
-            send(("gx", direction, h, e), ref, ref, at_x(1 if direction == 0 else 7))
+    def gather_out(e):
+        ref = x_part(x, e)
+        for step in (2, 1):
+            for direction in (0, 1):
+                send(("gx", direction, step, e), ref, ref, at_x(step if direction == 0 else NX - step))
+
+    def gather_on(direction, e):
+        ref = x_part(origin(2, direction), e)
+        arrived(("gx", direction, 2, e), ref)
+        for step in (2, 1) if e in LAST[direction] else (1,):
+            send(("gx", direction, 2 + step, e), ref, ref, at_x(step if direction == 0 else NX - step))
+
+    def gather_end(h, direction):
+        for e in PARTS:
+            arrived(("gx", direction, h, e), x_part(origin(h, direction), e))
+        gather_core(h, direction)
 
     def gather_core(h, direction):
         ref = x_all(origin(h, direction))
@@ -222,8 +232,7 @@
     y_block = x_part(x, 0)
     for d in (1, 7, 2):
         send(("gy", d), y_block, y_block, at_ring_y(d))
-    for direction in (0, 1):
-        gather_x(0, direction, 0)
+    gather_out(0)
 
     for i in (3, 4, 5):
         local[i].wait()
@@ -258,8 +267,7 @@
 
     for d, e in ((7, 1), (1, 3), (2, 2)):
         arrived(("gy", d), x_part(x, e))
-        for direction in (0, 1):
-            gather_x(0, direction, e)
+        gather_out(e)
     gather_core(0, 0)
 
     arrived(("pair", 1), precv.at[1])
@@ -268,14 +276,11 @@
         hop(3, 0, up_e)
         hop(3, 1, down_e)
 
-    def gather_step(h):
-        for e in PARTS:
-            gather_x(h, 0, e)
-            gather_x(h, 1, e)
-        gather_core(h, 0)
-        gather_core(h, 1)
-
-    gather_step(1)
+    for e in PARTS:
+        gather_on(0, e)
+        gather_on(1, e)
+    gather_core(2, 0)
+    gather_core(2, 1)
 
     arrived(("pair", 0), precv.at[0])
 
@@ -306,7 +311,8 @@
         send(("y", e), ysend.at[e], yrecv.at[e], at_y(e))
     grad = ysums[3][1]
 
-    gather_step(2)
+    gather_end(1, 0)
+    gather_end(1, 1)
 
     scale = float(GROUP_TOK) ** -0.5
     arrived(("old",), cmom.at[0])
@@ -321,8 +327,14 @@
     for d in (4, 3, 5, 2, 6, 1, 7):
         send(("rep", d), c2r.at[x], c2r.at[x], at_x(d))
 
-    gather_step(3)
-
+    gather_end(3, 0)
+    gather_end(3, 1)
+
+    far = lax.rem(x + 4, NX)
+    for direction in (0, 1):
+        for e in LAST[direction]:
+            arrived(("gx", direction, 4, e), x_part(far, e))
+    send(("gc", 0, 4), x_all(far), x_all(far), sibling)
     for e in LATE[:3]:
         arrived(("y", e), yrecv.at[e])
         grad = grad + yrecv[e].astype(F32)
@@ -340,11 +352,6 @@
         c.wait_send()
     del started[:-15]
 
-    far = lax.rem(x + 4, NX)
-    for direction in (0, 1):
-        for e in LAST[direction]:
-            arrived(("gx", direction, 3, e), x_part(far, e))
-    send(("gc", 0, 4), x_all(far), x_all(far), sibling)
     for key in [("gc", 0, h) for h in range(5)] + [("gc", 1, h) for h in range(1, 4)]:
         arrived(key, x_all(x))
 
@@ -380,9 +387,9 @@
 
 
 def finish(ig, nm, up, nw, ig_out, nm_out, up_out, nw_out, ig_v, nm_v, up_v, nw_v, sems):
-    moves = [(nm, nm_v, nm_out), (up, up_v, up_out), (nw, nw_v, nw_out)]
     rows = ig.shape[0] // 4
-    moves += [tuple(r.at[rows * i:rows * i + rows] for r in (ig, ig_v, ig_out)) for i in range(4)]
+    moves = [tuple(r.at[rows * i:rows * i + rows] for r in (ig, ig_v, ig_out)) for i in range(4)]
+    moves += [(nm, nm_v, nm_out), (up, up_v, up_out), (nw, nw_v, nw_out)]
     loads = [pltpu.make_async_copy(src, mid, sems.at[0, i]) for i, (src, mid, _) in enumerate(moves)]
     stores = [pltpu.make_async_copy(mid, dst, sems.at[1, i]) for i, (_, mid, dst) in enumerate(moves)]
     for c in loads:

time: 57.3 us -> 56.9 us (level)
  the two profiles are of different devices: /device:TPU:1 before, /device:TPU:2 now
where the time goes in v4:
time: 56.9 us; the launch traced here: 56.7 us
  Pallas kernels  56 us (98%)
  between operations  0.64 us (1%)
    pallas_call x1, Pallas kernels, on_device(): pl.pallas_call(body, out_shape=shapes, in_specs=[hbm] * 6, out_specs=(hbm...  53.7 us
    pallas_call x1, Pallas kernels, on_device(): pl.pallas_call(finish, out_shape=shapes, in_specs=[hbm] * 4, out_specs=(h...  2.31 us

profile of v4, /device:TPU:2, one launch (start us, length us, event | category | flops | bytes accessed | tf_op | source)
XLA Modules:
  0.0 56.7 jit_solution(14285347022515436257)
XLA Ops:
  0.6 53.7 %demo_step.1 = (bf16[192,4096]{1,0:T(8,128)(2,1)}, f32[1,64,256]{2,1,0:T(8,128)}, f32[64,256]{1,0:T(8,128)}, f32[64,256]{1,0:T(8,128)}) custom-call(s32[64]{0:T(128)} %order_hbm.1, bf16[192,4096]{1,0:T(8,128)(2,1)} %tok_hbm.1, bf16[192,256]{1,0:T(8,128)(2,1)} %cot_hbm.1, f32[64,256]{1,0:T(8,128)} %weight_hbm.1, f32[1,64,256]{2,1,0:T(8,128)} %mom_hbm.1, ...), custom_call_target="tpu_custom_call" | custom-call | tf_op jit(solution)/shard_map/demo_step/pallas_call | solution.py:413
  54.4 2.3 %store_results.1 = (bf16[192,4096]{1,0:T(8,128)(2,1)}, f32[1,64,256]{2,1,0:T(8,128)}, f32[64,256]{1,0:T(8,128)}, f32[64,256]{1,0:T(8,128)}) custom-call(bf16[192,4096]{1,0:T(8,128)(2,1)} %get-tuple-element.8.ig, f32[1,64,256]{2,1,0:T(8,128)} %get-tuple-element.9.nm, f32[64,256]{1,0:T(8,128)} %get-tuple-element.10.up, f32[64,256]{1,0:T(8,128)} %get-tuple-element.11.nw), custom_call_target="tpu_custom_call" | custom-call | tf_op jit(solution)/shard_map/store_results/pallas_call | solution.py:446
